TPU v7x, 32 devices: a whole 2x2x4 slice. The times are simulated.
32 devices in a mesh: group: 4 (over y, x), dp: 8 (over z, core).
Axes of the slice: x: 2, y: 2, z: 4, core: 2. Of those that a mesh axis runs over, the one named last changes fastest.
Arguments:
- hidden: bfloat16 [8192, 2048], P(('group', 'dp')), may hold values from 0 to 40, as said below
- weight: bfloat16 [2048, 1024], replicated, may hold values from -0.125 to 0.125
- partners: int32 [32, 256], P(('group', 'dp')), may hold values from 0 to 255, each once within a row
Outputs:
- whitened: bfloat16 [8192, 1024], P(('group', 'dp'))
- grad_weight: float32 [2048, 1024], P(('group', 'dp'))
- grad_hidden: bfloat16 [8192, 2048], P(('group', 'dp'))
Inputs may be any that keep to these rules, and one draw needn't show every extreme that they name: `hidden`: nonnegative activations. `partners`: each row is a permutation of 0 to 255.
All inputs are finite; a program needn't handle non-finite values.
Results may differ from a plain program's by a relative error of at most 0.0089.
Values sent between devices are 32-bit elements; how exact they have to be, the bound alone decides.
No kernel may reach another device: no remote copies, remote signals or barrier semaphores. Data moves between devices by JAX's collectives and lax.ppermute only.
A program may use at most 128 MiB of HBM per device.

v0:
```python
import jax
import jax.numpy as jnp
from jax import lax
from jax.sharding import PartitionSpec as P

epsilon = 1e-06
highest = lax.Precision.HIGHEST


def body(hidden, weight, partners):
    local_rows = hidden.shape[0]
    total_rows = local_rows * lax.axis_size("group") * lax.axis_size("dp")
    embedded = jnp.dot(hidden, weight, preferred_element_type=jnp.float32)
    mean_row = lax.psum(jnp.sum(embedded, axis=0), ("group", "dp")) / total_rows
    centered = embedded - mean_row
    scatter = lax.psum(jnp.dot(centered.T, centered, precision=highest), ("group", "dp"))
    cov = scatter / (total_rows - 1)
    factor = jnp.linalg.cholesky(cov)
    white = lax.linalg.triangular_solve(
        factor, centered, left_side=False, lower=True, transpose_a=True
    )
    whitened = white.astype(jnp.bfloat16)
    row_norm = jnp.sqrt(jnp.sum(white * white, axis=1, keepdims=True) + epsilon)
    unit = white / row_norm
    partner = partners[0]
    row_ids = jnp.arange(local_rows, dtype=jnp.int32)
    inverse = jnp.zeros((local_rows,), jnp.int32).at[partner].set(row_ids)
    grad_unit = 2.0 * (
        2.0 * unit - jnp.take(unit, partner, axis=0) - jnp.take(unit, inverse, axis=0)
    )
    inner_prod = jnp.sum(white * grad_unit, axis=1, keepdims=True)
    grad_white = grad_unit / row_norm - white * (inner_prod / row_norm**3)
    local_pair = jnp.dot(grad_white.T, white, precision=highest)
    direct = lax.linalg.triangular_solve(
        factor, grad_white, left_side=False, lower=True, transpose_a=False
    )
    pair_moment = lax.psum(local_pair, ("group", "dp"))
    lower_half = -(jnp.tril(pair_moment) - 0.5 * jnp.diag(jnp.diag(pair_moment)))
    left_solved = lax.linalg.triangular_solve(
        factor, lower_half, left_side=True, lower=True, transpose_a=True
    )
    solved = lax.linalg.triangular_solve(
        factor, left_solved, left_side=False, lower=True, transpose_a=False
    )
    grad_cov = 0.5 * (solved + solved.T)
    grad_cent = direct + 2.0 / (total_rows - 1) * jnp.dot(centered, grad_cov, precision=highest)
    column_sums = lax.psum(jnp.sum(grad_cent, axis=0), ("group", "dp"))
    grad_z = (grad_cent - column_sums / total_rows).astype(jnp.bfloat16)
    grad_hidden = jnp.dot(grad_z, weight.T, preferred_element_type=jnp.float32).astype(jnp.bfloat16)
    grad_weight = lax.psum_scatter(
        lax.dot_general(
            hidden, grad_z, (((0,), (0,)), ((), ())), preferred_element_type=jnp.float32
        ),
        ("group", "dp"),
        scatter_dimension=0,
        tiled=True,
    )
    return (whitened, grad_weight, grad_hidden)


def solution(mesh):
    return jax.shard_map(
        body,
        mesh=mesh,
        in_specs=(P(("group", "dp"), None), P(), P(("group", "dp"), None)),
        out_specs=(P(("group", "dp"), None), P(("group", "dp"), None), P(("group", "dp"), None)),
        check_vma=False,
    )
```

profile of v0, /device:TPU:0, one launch (start us, length us, event | category | flops | bytes accessed | tf_op | source)
XLA Modules:
  0.0 1027.2 jit_solution(11250101548871496075)
XLA Ops:
  11.8 42.0 %psum.28 = f32[1024]{0:T(1024)S(1)} all-reduce(f32[1024]{0:T(1024)S(1)} %get-tuple-element.80), channel_id=1, replica_groups=mesh['group'=4,'dp'=8] {'group','dp'}, use_global_device_ids=true, to_apply=%region_1.0 | all-reduce | flops 1024 | bytes 8192 | tf_op jit(solution)/shard_map/psum | solution.py:14
  54.1 5.2 fusion.194
  60.8 140.1 %all-reduce.4.cloned.1.call-done = f32[1024,1024]{0,1:T(8,128)} async-done(((f32[1024,1024]{0,1:T(8,128)}), f32[1024,1024]{0,1:T(8,128)}) %all-reduce.4.cloned.1.call-update) | async-done | bytes 4194320 | tf_op jit(solution)/shard_map/psum | solution.py:16
  201.0 5.1 broadcast_multiply_fusion
  206.0 5.8 copy.27
  218.3 11.7 %cholesky.223 = f32[128,128]{1,0:T(8,128)S(1)} custom-call(f32[128,128]{1,0:T(8,128)S(1)} %cholesky.580), custom_call_target="Cholesky" | custom-call | tf_op jit(solution)/shard_map/jit(cholesky)/cholesky | solution.py:18
  230.0 9.8 custom-call.68
  246.3 11.8 %cholesky.244 = f32[128,128]{1,0:T(8,128)S(1)} custom-call(f32[128,128]{1,0:T(8,128)S(1)} %cholesky.584), custom_call_target="Cholesky" | custom-call | tf_op jit(solution)/shard_map/jit(cholesky)/cholesky | solution.py:18
  258.8 9.8 custom-call.69
  272.0 11.7 %cholesky.468 = f32[128,128]{1,0:T(8,128)S(1)} custom-call(f32[128,128]{1,0:T(8,128)S(1)} %cholesky.589), custom_call_target="Cholesky" | custom-call | tf_op jit(solution)/shard_map/jit(cholesky)/cholesky | solution.py:18
  284.9 9.8 custom-call.70
  298.3 11.9 %cholesky.487 = f32[128,128]{1,0:T(8,128)S(1)} custom-call(f32[128,128]{1,0:T(8,128)S(1)} %cholesky.594), custom_call_target="Cholesky" | custom-call | tf_op jit(solution)/shard_map/jit(cholesky)/cholesky | solution.py:18
  311.5 9.8 custom-call.71
  324.8 11.7 %cholesky.506 = f32[128,128]{1,0:T(8,128)S(1)} custom-call(f32[128,128]{1,0:T(8,128)S(1)} %cholesky.599), custom_call_target="Cholesky" | custom-call | tf_op jit(solution)/shard_map/jit(cholesky)/cholesky | solution.py:18
  337.8 10.2 custom-call.72
  351.3 11.7 %cholesky.526 = f32[128,128]{1,0:T(8,128)S(1)} custom-call(f32[128,128]{1,0:T(8,128)S(1)} %cholesky.604), custom_call_target="Cholesky" | custom-call | tf_op jit(solution)/shard_map/jit(cholesky)/cholesky | solution.py:18
  364.3 9.8 custom-call.73
  377.1 11.8 %cholesky.546 = f32[128,128]{1,0:T(8,128)S(1)} custom-call(f32[128,128]{1,0:T(8,128)S(1)} %cholesky.609), custom_call_target="Cholesky" | custom-call | tf_op jit(solution)/shard_map/jit(cholesky)/cholesky | solution.py:18
  390.2 9.8 custom-call.74
  402.6 11.7 %cholesky.564 = f32[128,128]{1,0:T(8,128)S(1)} custom-call(f32[128,128]{1,0:T(8,128)S(1)} %convolution_subtract_fusion.30), custom_call_target="Cholesky" | custom-call | tf_op jit(solution)/shard_map/jit(cholesky)/cholesky | solution.py:18
  426.1 27.9 %while.1 = (s32[]{:T(128)}, f32[1024,1024]{1,0:T(8,128)}, s32[8,2]{0,1:T(2,128)S(1)}, f32[8,128,128]{2,1,0:T(8,128)}, s32[]{:T(128)}) while((s32[]{:T(128)}, f32[1024,1024]{1,0:T(8,128)}, s32[8,2]{0,1:T(2,128)S(1)}, f32[8,128,128]{2,1,0:T(8,128)}, s32[]{:T(128)}) %tuple.79), condition=%wide.while_cond, body=%wide.while_body.sunk | while | flops 2 | bytes 132205 | solution.py:19
  454.0 80.2 %custom-call.75 = f32[8,128,128]{1,2,0:T(8,128)} custom-call(f32[8,128,128]{2,1,0:T(8,128)} %get-tuple-element.11), custom_call_target="InvertDiagBlocksLowerTriangular" | custom-call | tf_op jit(solution)/shard_map/triangular_solve | solution.py:19
  569.5 5.5 fusion.195
  593.9 132.9 %all-reduce.6.cloned.1.call-done = f32[1024,1024]{1,0:T(8,128)} async-done(((f32[1024,1024]{1,0:T(8,128)}), f32[1024,1024]{1,0:T(8,128)}) %all-reduce.6.cloned.1.call-update) | async-done | bytes 4194320 | tf_op jit(solution)/shard_map/psum | solution.py:37
  726.8 17.3 %gather_fusion = f32[1024]{0:T(1024)S(1)} fusion(f32[1024,1024]{1,0:T(8,128)} %all-reduce.6.cloned.1.call-done, s32[1024]{0:T(1024)S(1)} %bitcast.205), kind=kCustom, calls=%fused_computation.2 | custom fusion | bytes 16384 | tf_op jit(solution)/shard_map/jit(_diag)/jit(diagonal)/cond/branch_0_fun/gather | solution.py:38
  781.0 5.2 convolution_subtract_fusion.2
  787.1 5.9 convolution_subtract_fusion.6
  800.4 5.4 copy.39
  805.9 10.0 fusion.193
  815.9 39.1 %psum.31 = f32[1024]{0:T(1024)S(1)} all-reduce(f32[1024]{0:T(1024)S(1)} %get-tuple-element.106), channel_id=1, replica_groups=mesh['group'=4,'dp'=8] {'group','dp'}, use_global_device_ids=true, to_apply=%region_24.26 | all-reduce | flops 1024 | bytes 8192 | tf_op jit(solution)/shard_map/psum | solution.py:47
  859.5 9.3 copy.52
  875.5 144.9 %reduce-scatter.4.cloned.1.call-done = f32[64,1024]{1,0:T(8,128)} async-done(((f32[2048,1024]{1,0:T(8,128)}), f32[64,1024]{1,0:T(8,128)}) %reduce-scatter.4.cloned.1.call-update) | async-done | bytes 262160
  (243 shorter events, 189.8 us)
Async XLA Ops:
  7.2 1.2 copy-start
  7.2 193.8 %all-reduce.4.cloned.1.call-start = ((), (), s32[]{:S(2)}) async-start(), calls=%async_computation.1 | async-start | bytes 8388608 | tf_op jit(solution)/shard_map/psum | solution.py:16
  54.0 496.2 %copy-start.2 = (f32[256,1024]{1,0:T(8,128)}, f32[256,1024]{1,0:T(8,128)S(1)}, u32[]{:S(2)}) copy-start(f32[256,1024]{1,0:T(8,128)S(1)} %broadcast_subtract_fusion) | copy-start | bytes 3145732
  54.0 5.3 copy-start.9
  59.3 667.5 %all-reduce.6.cloned.1.call-start = ((), (), s32[]{:S(2)}) async-start(), calls=%async_computation.2 | async-start | bytes 8388608 | tf_op jit(solution)/shard_map/psum | solution.py:37
  216.4 1.9 copy-start.4
  534.2 8.1 copy-start.6
  568.2 1.3 copy-start.5
  568.2 8.0 copy-start.7
  585.9 434.5 %reduce-scatter.4.cloned.1.call-start = ((), (), s32[]{:S(2)}) async-start(), calls=%async_computation.3 | async-start | bytes 8650752
  744.1 3.6 copy-start.1
  800.4 5.4 copy-start.3
  868.8 1.0 copy-start.8
Sparse Core Ops, SparseCore 0:
  59.4 141.5 all-reduce.3
  586.0 140.7 all-reduce.5
  868.9 151.4 reduce-scatter.3
where the time goes:
time: 1030 us
  waiting for transfers between devices  418 us (41%)
  other arithmetic  275 us (27%)
  matrix products  136 us (13%)
  local copies, waits for them, and re-layouts  96.8 us (9%)
  blocking collectives  81.1 us (8%)
  between operations  20.1 us (2%)
    another operation x30, other arithmetic, body(): factor = jnp.linalg.cholesky(cov)  172 us
    unnamed x4, waiting for transfers between devices  145 us
    psum x1, waiting for transfers between devices, body(): lax.psum(jnp.dot(centered.T, centered, precision=highest), ('group', 'dp'))  140 us
    psum x1, waiting for transfers between devices, body(): pair_moment = lax.psum(local_pair, ('group', 'dp'))  133 us
    another operation x3, other arithmetic, body(): lax.linalg.triangular_solve(factor, centered, left_side=False, lower=True...  85 us
    psum x1, blocking collectives, body(): mean_row = lax.psum(jnp.sum(embedded, axis=0), ('group', 'dp')) / total_rows  42 us
    psum x1, blocking collectives, body(): column_sums = lax.psum(jnp.sum(grad_cent, axis=0), ('group', 'dp'))  39.1 us
    another operation x15, matrix products, body(): lax.linalg.triangular_solve(factor, left_solved, left_side=False, lower=T...  30.5 us
  transfers between devices with their start and end apart: 3, of which 3 were waited for; matrix products, arithmetic and copies ran while one was open for 1% of the time, Pallas kernels for 0%

commit v1 on v0

v1 whole, which is shorter than its diff:
```python
import functools

import jax
import jax.numpy as jnp
from jax import lax
from jax.experimental import pallas as pl
from jax.experimental.pallas import tpu as pltpu
from jax.sharding import PartitionSpec as P

AXES = ("group", "dp")
epsilon = 1e-06
f32 = jnp.float32
bf16 = jnp.bfloat16
NN = (((1,), (0,)), ((), ()))
NT = (((1,), (1,)), ((), ()))
TN = (((0,), (0,)), ((), ()))
BLK = 128
PANEL = 32
VMEM = pl.BlockSpec(memory_space=pltpu.VMEM)
SMEM = pl.BlockSpec(memory_space=pltpu.SMEM)
PARAMS = pltpu.CompilerParams(vmem_limit_bytes=50 * 2**20)


def split2(x):
    high = x.astype(bf16)
    return high, (x - high.astype(f32)).astype(bf16)


def split3(x):
    high = x.astype(bf16)
    rest = x - high.astype(f32)
    mid = rest.astype(bf16)
    return high, mid, (rest - mid.astype(f32)).astype(bf16)


def left6(parts, axis):
    high, mid, low = parts
    return jnp.concatenate([high, high, mid, high, low, mid], axis=axis)


def right6(parts, axis):
    high, mid, low = parts
    return jnp.concatenate([high, mid, high, low, high, mid], axis=axis)


def left3(parts, axis):
    return jnp.concatenate([parts[0], parts[0], parts[1]], axis=axis)


def right3(parts, axis):
    return jnp.concatenate([parts[0], parts[1], parts[0]], axis=axis)


def mm(a, b, dims):
    return lax.dot_general(a, b, dims, preferred_element_type=f32)


def dot6(a, b, dims):
    (ca,), (cb,) = dims[0]
    return mm(left6(split3(a), ca), right6(split3(b), cb), dims)


def dot3(a, b, dims):
    (ca,), (cb,) = dims[0]
    return mm(left3(split2(a), ca), right3(split2(b), cb), dims)


def starts(blocks):
    out, at = [], 0
    for j in range(blocks):
        out.append(at)
        at += (blocks - j) * BLK
    return out, at


def radices(count):
    out = []
    while count > 1:
        out.append(4 if count % 4 == 0 else 2)
        count //= out[-1]
    return out


def rounds():
    groups, per = lax.axis_size("group"), lax.axis_size("dp")
    out, at = [(1, 2)], per
    for radix in radices(groups):
        out.append((at, radix))
        at *= radix
    at = 2
    for radix in radices(per // 2):
        out.append((at, radix))
        at *= radix
    return out


def place():
    index = lax.axis_index("group") * lax.axis_size("dp") + lax.axis_index("dp")
    out = 0
    for stride, radix in rounds():
        out = out * radix + (index // stride) % radix
    return out.astype(jnp.int32).reshape(1, 1)


def owner(position):
    index = 0
    for stride, radix in reversed(rounds()):
        index = index + (position % radix) * stride
        position = position // radix
    return index


def swap(x, stride, by):
    count = lax.axis_size("group") * lax.axis_size("dp")
    return lax.ppermute(x, AXES, [(i, i ^ (by * stride)) for i in range(count)])


def combine_kernel(size, extra, listed, parts, radix, *refs):
    ins, outs = refs[:parts], refs[parts:]
    total = ins[0][0:size, :]
    for r in ins[1:]:
        total = total + r[0:size, :]
    if listed:
        more = jnp.concatenate([r[size : size + extra, :] for r in ins], 0)
    else:
        more = ins[0][size : size + extra, :]
        for r in ins[1:]:
            more = more + r[size : size + extra, :]
    if radix == 1:
        outs[0][...] = total
        outs[1][...] = more
        return
    cut = size // radix
    for i, out in enumerate(outs):
        out[0:cut, :] = total[i * cut : (i + 1) * cut, :]
        out[cut:, :] = more


def reduce_scatter(keep, send, size, extra, listed):
    steps = rounds()
    pieces = [keep, send]
    for at, (stride, radix) in enumerate(steps):
        ins = [pieces[0]] + [swap(p, stride, by) for by, p in enumerate(pieces) if by]
        after = steps[at + 1][1] if at + 1 < len(steps) else 1
        more = extra * radix if listed else extra
        shapes = [(size // after + more, BLK)] * after if after > 1 else [(size, BLK), (more, BLK)]
        pieces = call(
            functools.partial(combine_kernel, size, extra, listed, len(ins), after),
            [(s, f32) for s in shapes],
            *ins,
        )
        extra, size = more, size // after
    return pieces


def all_gather(x):
    steps = rounds()
    parts = [x]
    for at in range(len(steps) - 1, 0, -1):
        stride, radix = steps[at]
        whole = parts[0] if len(parts) == 1 else jnp.concatenate(parts, 0)
        parts = [whole] + [swap(whole, stride, by) for by in range(1, radix)]
    return parts + [swap(p, 1, 1) for p in parts]


def padded(rows):
    unit = 8 * lax.axis_size("group") * lax.axis_size("dp")
    return -(-rows // unit) * unit


def gather_into(pos, parts, out_ref, devices):
    chunk = out_ref.shape[0] // devices
    each = devices // len(parts)
    for i, part in enumerate(parts):
        for j in range(each):
            to = pl.multiple_of(((i * each + j) ^ pos) * chunk, 8)
            out_ref[pl.ds(to, chunk), :] = part[j * chunk : (j + 1) * chunk, :]


def scatter_from(pos, src_ref, keep_ref, send_ref, devices):
    chunk = src_ref.shape[0] // devices
    half = devices // 2
    for i in range(devices):
        at = pl.multiple_of((i ^ pos) * chunk, 8)
        out = keep_ref if i < half else send_ref
        out[(i % half) * chunk : (i % half + 1) * chunk, :] = src_ref[pl.ds(at, chunk), :]


def put_row(out_ref, at, row):
    for i in range(row.shape[1] // BLK):
        out_ref[at + i : at + i + 1, :] = row[:, i * BLK : (i + 1) * BLK]


def get_row(ref, at, blocks):
    return jnp.concatenate([ref[at + i : at + i + 1, :] for i in range(blocks)], 1)


def lower_products(a, b, out_ref, blocks):
    at, total = starts(blocks)
    left, right = left6(split3(a), 0), right6(split3(b), 0)
    for j in range(blocks):
        rows = (blocks - j) * BLK
        out_ref[at[j] : at[j] + rows, :] = mm(left[:, j * BLK :], right[:, j * BLK : (j + 1) * BLK], TN)
    if out_ref.shape[0] > total:
        out_ref[total:, :] = jnp.zeros((out_ref.shape[0] - total, BLK), f32)


def front_kernel(blocks, devices, pos_ref, hid_ref, w_ref, emb_ref, keep_ref, send_ref, pay_ref):
    emb = mm(hid_ref[...], w_ref[...], NN)
    emb_ref[...] = emb
    total = jnp.sum(emb, axis=0, keepdims=True)
    cent = emb - total / emb.shape[0]
    lower_products(cent, cent, pay_ref, blocks)
    scatter_from(pos_ref[0, 0], pay_ref, keep_ref, send_ref, devices)
    half = pay_ref.shape[0] // 2
    put_row(keep_ref, half, total)
    put_row(send_ref, half, total)


def turn_kernel(places, pos_ref, hid_ref, keep_a, keep_b, send_a, send_b, turned_ref, part_ref):
    turned_ref[...] = hid_ref[...].astype(f32).T
    pos = pos_ref[0, 0]
    groups, rest = lax.axis_size("group"), lax.axis_size("dp") // 2
    own = turned_ref.shape[0] // (2 * groups * rest)
    for core, outs in enumerate(((keep_a, keep_b), (send_a, send_b))):
        for order, out in zip(places, outs):
            for i, g in enumerate(order):
                for z in range(rest):
                    device = owner(((core * groups + g) * rest + z) ^ pos)
                    rows = turned_ref[pl.ds(pl.multiple_of(device * own, 8), own), :]
                    part_ref[(i * rest + z) * own : (i * rest + z + 1) * own, :] = rows
            out[...] = part_ref[...].astype(bf16)


def lane(x, c):
    return jnp.broadcast_to(x[:, c : c + 1], (x.shape[0], BLK))


def sub(x, i):
    return jnp.broadcast_to(x[i : i + 1, :], (8, x.shape[1]))


def eye():
    shape = (BLK, BLK)
    return (lax.broadcasted_iota(jnp.int32, shape, 0) == lax.broadcasted_iota(jnp.int32, shape, 1)).astype(f32)


def inverse_factor(s):
    row = lax.broadcasted_iota(jnp.int32, (8, BLK), 0)
    t = eye()
    count = PANEL // 8
    outs = []
    for at in range(0, BLK, PANEL):
        r = [s[8 * q : 8 * q + 8] for q in range(count)]
        v = [t[8 * q : 8 * q + 8] for q in range(count)]
        done_r, done_v = [], []
        for p in range(count):
            col = at + 8 * p
            a = {q: [lane(r[q], col + l) for l in range(8)] for q in range(p, count)}
            pivots = jnp.ones((8, BLK), f32)
            for i in range(8):
                piv = [sub(a[p][l], i) for l in range(i, 8)]
                inv = 1.0 / piv[0]
                pivots = jnp.where(row == i, piv[0], pivots)
                rs, vs = sub(r[p], i), sub(v[p], i)
                for q in range(p, count):
                    if q == p and i == 7:
                        continue
                    m = a[q][i] * inv
                    if q == p:
                        m = jnp.where(row > i, m, 0.0)
                    for l in range(i + 1, 8):
                        a[q][l] = a[q][l] - m * piv[l - i]
                    r[q] = r[q] - m * rs
                    v[q] = v[q] - m * vs
            scale = lax.rsqrt(pivots)
            done_r.append(r[p] * scale)
            done_v.append(v[p] * scale)
        u, w = jnp.concatenate(done_r, 0), jnp.concatenate(done_v, 0)
        outs.append(w)
        if at + PANEL < BLK:
            us, ws = split3(u), split3(w)
            right = jnp.concatenate([right6(us, 0), right6(ws, 0)], axis=1)
            update = mm(left6(us, 0), right, TN)
            s = s[PANEL:] - update[at + PANEL :, :BLK]
            t = t[PANEL:] - update[at + PANEL :, BLK:]
    return jnp.concatenate(outs, 0)


def factor_kernel(blocks, total_rows, devices, parts, *refs):
    pos_ref, sums_ref, emb_ref, partner_ref = refs[:4]
    part_refs = refs[4 : 4 + parts]
    xt_ref, white_ref, out_ref, grad_ref, keep_ref, send_ref, a_ref, pay_ref = refs[4 + parts :]
    pos = pos_ref[0, 0]
    gather_into(pos, part_refs, pay_ref, devices)
    n = blocks * BLK
    local = emb_ref.shape[0]
    at, _ = starts(blocks)
    sums = jnp.concatenate([sums_ref[pl.ds(j, devices, blocks), :] for j in range(blocks)], 1)
    mean = jnp.sum(sums, axis=0, keepdims=True) / total_rows
    apart = sums / local - mean
    left, right = left6(split3(apart), 0), right6(split3(apart), 0)
    for j in range(blocks):
        lo, hi = j * BLK, (j + 1) * BLK
        between = mm(left[:, lo:], right[:, lo:hi], TN)
        a_ref[j, lo:n, :] = (pay_ref[at[j] : at[j] + n - lo, :] + local * between) / (total_rows - 1)
        a_ref[j, n:, :] = emb_ref[:, lo:hi] - mean[:, lo:hi]
        if j:
            a_ref[j, 0:lo, :] = jnp.zeros((lo, BLK), f32)
    one = eye()

    def step(k, _):
        lo = pl.ds(pl.multiple_of(k * BLK, BLK), BLK)
        x = inverse_factor(a_ref[k, lo, :])
        a_ref[k, lo, :] = one
        panel = dot6(a_ref[k], x, NT)
        a_ref[k] = panel
        left = left6(split3(panel), 1)

        def update(j, _):
            here = pl.ds(pl.multiple_of(j * BLK, BLK), BLK)
            right = right6(split3(a_ref[k, here, :]), 1)
            a_ref[j, lo, :] = jnp.zeros((BLK, BLK), f32)
            a_ref[j] = a_ref[j] - mm(left, right, NT)
            return 0

        lax.fori_loop(k + 1, blocks, update, 0)
        return 0

    lax.fori_loop(0, blocks, step, 0)
    for j in range(blocks):
        lo, hi = j * BLK, (j + 1) * BLK
        xt_ref[0:hi, lo:hi] = a_ref[j, 0:hi, :]
        if hi < n:
            xt_ref[hi:, lo:hi] = jnp.zeros((n - hi, BLK), f32)
        white_ref[:, lo:hi] = a_ref[j, n:, :]


    white = white_ref[...]
    rows = white.shape[0]
    out_ref[...] = white.astype(bf16)
    norm = jnp.sqrt(jnp.sum(white * white, axis=1, keepdims=True) + epsilon)
    unit = white / norm
    hit = (lax.broadcasted_iota(jnp.int32, (rows, rows), 0) == partner_ref[...]).astype(f32)
    pairs = (hit + hit.T).astype(bf16)
    parts = split3(unit)
    near = mm(jnp.concatenate([pairs] * 3, 1), jnp.concatenate(parts, 0), NN)
    grad_unit = 2.0 * (2.0 * unit - near)
    inner = jnp.sum(white * grad_unit, axis=1, keepdims=True)
    grad = grad_unit / norm - white * (inner / (norm * norm * norm))
    grad_ref[...] = grad
    lower_products(grad, white, pay_ref, blocks)
    scatter_from(pos, pay_ref, keep_ref, send_ref, devices)
    half = pay_ref.shape[0] // 2
    for i, rows in enumerate((grad, white)):
        total = jnp.sum(rows, axis=0, keepdims=True)
        put_row(keep_ref, half + i * blocks, total)
        put_row(send_ref, half + i * blocks, total)


def moment_product(rows, pay_ref, blocks):
    n = blocks * BLK
    at, _ = starts(blocks)
    below = lax.broadcasted_iota(jnp.int32, (BLK, BLK), 0) > lax.broadcasted_iota(jnp.int32, (BLK, BLK), 1)
    parts = split2(rows)
    outs = [None] * blocks
    for j in range(blocks):
        lo = j * BLK
        block = pay_ref[at[j] : at[j] + BLK, :]
        strict = jnp.where(below, block, 0.0)
        column = jnp.where(eye() > 0, block, 0.0) + strict + strict.T
        if j + 1 < blocks:
            column = jnp.concatenate([column, pay_ref[at[j] + BLK : at[j] + n - lo, :]], 0)
        part = mm(left3([p[:, lo:] for p in parts], 1), right3(split2(column), 0), NN)
        outs[j] = part if outs[j] is None else outs[j] + part
        if j + 1 < blocks:
            part = mm(left3([p[:, lo : lo + BLK] for p in parts], 1), right3(split2(column[BLK:]), 1), NT)
            for i in range(j + 1, blocks):
                add = part[:, (i - j - 1) * BLK : (i - j) * BLK]
                outs[i] = add if outs[i] is None else outs[i] + add
    return jnp.concatenate(outs, 1)


def back_kernel(blocks, total_rows, devices, parts, *refs):
    pos_ref, sums_ref, grad_ref, white_ref, xt_ref = refs[:5]
    part_refs = refs[5 : 5 + parts]
    out_ref, pay_ref = refs[5 + parts :]
    gather_into(pos_ref[0, 0], part_refs, pay_ref, devices)
    n = blocks * BLK
    rows = jnp.concatenate([white_ref[...], jnp.broadcast_to(get_row(sums_ref, blocks, blocks), (8, n))], 0)
    firsts = jnp.concatenate([grad_ref[...], jnp.broadcast_to(get_row(sums_ref, 0, blocks), (8, n))], 0)
    left = firsts - moment_product(rows, pay_ref, blocks) / (total_rows - 1)
    cent = dot3(left, xt_ref[...], NT)
    local = grad_ref.shape[0]
    out_ref[...] = (cent[:local] - cent[local : local + 1, :] / total_rows).astype(bf16)


def call(kernel, outs, *args, scratch=()):
    return pl.pallas_call(
        kernel,
        out_shape=tuple(jax.ShapeDtypeStruct(s, t) for s, t in outs),
        in_specs=[SMEM if a.dtype == jnp.int32 and a.size == 1 else VMEM for a in args],
        out_specs=(VMEM,) * len(outs),
        scratch_shapes=list(scratch),
        compiler_params=PARAMS,
    )(*args)


def weight_sums(keep_a, keep_b, send_a, send_b, grad_z):
    groups, per = lax.axis_size("group"), lax.axis_size("dp")
    half = grad_z.shape[1] // 2
    own = keep_a.shape[0] // (groups * (per // 2))
    cols = (grad_z[:, :half], grad_z[:, half:])
    sent = [swap(mm(h, c, NN), 1, 1) for h, c in zip((send_a, send_b), cols)]
    kept = [mm(h, c, NN) for h, c in zip((keep_a, keep_b), cols)]
    steps = [1 << i for i in range(groups.bit_length() - 1)]
    for at in range(len(steps)):
        order = (steps[at:] + steps[:at], steps[::-1][at:] + steps[::-1][:at])
        size = kept[0].shape[0] // 2
        out = []
        for k, r, o in zip(kept, sent, order):
            out.append((k[:size] + r[:size], swap(k[size:] + r[size:], per, o[0])))
        kept, sent = [k for k, _ in out], [r for _, r in out]
    x = jnp.concatenate([k + r for k, r in zip(kept, sent)], 1)
    for stride, radix in rounds():
        if stride == 1 or stride >= per:
            continue
        size = x.shape[0] // radix
        got = [swap(x[by * size : (by + 1) * size], stride, by) for by in range(1, radix)]
        x = x[:size]
        for g in got:
            x = x + g
    return x


def group_orders(groups):
    def order(bits):
        out = [0]
        for bit in reversed(bits):
            out = out + [o | bit for o in out]
        return out

    bits = [1 << i for i in range(groups.bit_length() - 1)]
    return order(bits), order(bits[::-1])


def body(hidden, weight, partners):
    local, hid = hidden.shape
    emb = weight.shape[1]
    blocks = emb // BLK
    devices = lax.axis_size("group") * lax.axis_size("dp")
    total_rows = local * devices
    _, packed = starts(blocks)
    rows = padded(packed)
    half = rows // 2
    pos = place()
    pay_scratch = pltpu.VMEM((rows, BLK), f32)

    embedded, keep, send = call(
        functools.partial(front_kernel, blocks, devices),
        [((local, emb), f32), ((half + blocks, BLK), f32), ((half + blocks, BLK), f32)],
        pos,
        hidden,
        weight,
        scratch=[pay_scratch],
    )
    turned = call(
        functools.partial(turn_kernel, group_orders(lax.axis_size("group"))),
        [((hid // 2, local), bf16)] * 4,
        pos,
        hidden,
        scratch=[pltpu.VMEM((hid, local), f32), pltpu.VMEM((hid // 2, local), f32)],
    )
    part, sums = reduce_scatter(keep, send, half, blocks, True)
    parts = all_gather(part)
    xt, white, whitened, grad, keep, send = call(
        functools.partial(factor_kernel, blocks, total_rows, devices, len(parts)),
        [((emb, emb), f32), ((local, emb), f32), ((local, emb), bf16), ((local, emb), f32)]
        + [((half + 2 * blocks, BLK), f32)] * 2,
        pos,
        sums,
        embedded,
        partners,
        *parts,
        scratch=[pltpu.VMEM((blocks, emb + local, BLK), f32), pay_scratch],
    )
    part, sums = reduce_scatter(keep, send, half, 2 * blocks, False)
    parts = all_gather(part)
    (grad_z,) = call(
        functools.partial(back_kernel, blocks, total_rows, devices, len(parts)),
        [((local, emb), bf16)],
        pos,
        sums,
        grad,
        white,
        xt,
        *parts,
        scratch=[pay_scratch],
    )
    grad_weight = weight_sums(*turned, grad_z)
    grad_hidden = mm(grad_z, weight, NT).astype(bf16)
    return (whitened, grad_weight, grad_hidden)


def solution(mesh):
    return jax.shard_map(
        body,
        mesh=mesh,
        in_specs=(P(AXES, None), P(), P(AXES, None)),
        out_specs=(P(AXES, None), P(AXES, None), P(AXES, None)),
        check_vma=False,
    )
```

time: 1030 us -> 294 us (0.29)
  other arithmetic: 275 us -> 2.03 us
  waiting for transfers between devices: 418 us -> 151 us
  matrix products: 136 us -> 4.21 us
  local copies, waits for them, and re-layouts: 96.8 us -> 5.39 us
  Pallas kernels: 0 us -> 83.3 us
  blocking collectives: 81.1 us -> 0 us
  starting transfers between devices: 0.12 us -> 42.2 us
  between operations: 20.1 us -> 0.88 us
    psum x2 -> x0, waiting for transfers between devices: 273 us -> none  [the longest x1 140 us: body(): lax.psum(jnp.dot(centered.T, centered, precision=highest), ('group', 'dp'))]
    another operation x33 -> x0, other arithmetic: 257 us -> none  [the longest x30 172 us: body(): factor = jnp.linalg.cholesky(cov)]
    ppermute x0 -> x43, waiting for transfers between devices: none -> 151 us  [swap(): return lax.ppermute(x, AXES, [(i, i ^ by * stride) for i in range(count)])]
    unnamed x4 -> x0, waiting for transfers between devices: 145 us -> none
    another operation x74 -> x0, matrix products: 102 us -> none  [the longest x15 30.5 us: body(): lax.linalg.triangular_solve(factor, left_solved, left_side=False, lower=T...]
    pallas_call x0 -> x10, Pallas kernels: none -> 83.3 us  [call(): pl.pallas_call(kernel, out_shape=tuple((jax.ShapeDtypeStruct(s, t) for s,...]
    psum x2 -> x0, blocking collectives: 81.1 us -> none  [the longest x1 42 us: body(): mean_row = lax.psum(jnp.sum(embedded, axis=0), ('group', 'dp')) / total_rows]
    ppermute x0 -> x43, starting transfers between devices: none -> 42.2 us  [swap(): return lax.ppermute(x, AXES, [(i, i ^ by * stride) for i in range(count)])]
  transfers between devices with their start and end apart: 3 -> 43, of which waited for: 3 -> 31; matrix products, arithmetic and copies ran while one was open for 1% -> 2% of each run, Pallas kernels for 0% -> 0%
where the time goes in v1:
time: 294 us; the launch traced here: 289 us
  waiting for transfers between devices  151 us (51%)
  Pallas kernels  83.3 us (28%)
  starting transfers between devices  42.2 us (14%)
  local copies, waits for them, and re-layouts  5.39 us (2%)
  matrix products  4.21 us (1%)
    ppermute x43, waiting for transfers between devices, swap(): return lax.ppermute(x, AXES, [(i, i ^ by * stride) for i in range(count)])  151 us
    pallas_call x10, Pallas kernels, call(): pl.pallas_call(kernel, out_shape=tuple((jax.ShapeDtypeStruct(s, t) for s,...  83.3 us
    ppermute x43, starting transfers between devices, swap(): return lax.ppermute(x, AXES, [(i, i ^ by * stride) for i in range(count)])  42.2 us
  transfers between devices with their start and end apart: 43, of which 31 were waited for; matrix products, arithmetic and copies ran while one was open for 2% of the time, Pallas kernels for 0%

profile of v1, /device:TPU:0, one launch (start us, length us, event | category | flops | bytes accessed | tf_op | source)
XLA Modules:
  0.0 288.8 jit_solution(15181187807846425630)
XLA Ops:
  1.9 8.5 %shard_map.58 = (f32[256,1024]{1,0:T(8,128)S(1)}, f32[2312,128]{1,0:T(8,128)S(1)}, f32[2312,128]{1,0:T(8,128)}) custom-call(s32[1,1]{1,0:T(1,128)} %bitcast.pos_ref.refs_0_, bf16[256,2048]{1,0:T(8,128)(2,1)S(1)} %copy-done, bf16[2048,1024]{1,0:T(8,128)(2,1)} %w_ref.1), custom_call_target="tpu_custom_call" | custom-call | tf_op jit(solution)/shard_map/pallas_call | solution.py:399
  11.8 2.7 collective-permute-done.refs_1_
  14.7 2.9 %collective-permute-start.1 = (f32[592,128]{1,0:T(8,128)S(1)}, f32[592,128]{1,0:T(8,128)S(1)}, u32[]{:S(2)}, u32[]{:S(2)}) collective-permute-start(f32[592,128]{1,0:T(8,128)S(1)} %get-tuple-element.39), channel_id=1, source_target_pairs={{0,8},{1,9},{2,10},{3,11},{4,12},{5,13},{6,14},{7,15},{8,0},{9,1},... | collective-permute-start | bytes 909320 | tf_op jit(solution)/shard_map/ppermute | solution.py:115
  19.1 6.4 %collective-permute-done.1.refs_1_ = f32[592,128]{1,0:T(8,128)S(1)} collective-permute-done((f32[592,128]{1,0:T(8,128)S(1)}, f32[592,128]{1,0:T(8,128)S(1)}, u32[]{:S(2)}, u32[]{:S(2)}) %collective-permute-start.1) | collective-permute-done | bytes 303136 | tf_op jit(solution)/shard_map/ppermute | solution.py:115
  25.6 7.5 %collective-permute-done.2.refs_2_ = f32[592,128]{1,0:T(8,128)S(1)} collective-permute-done((f32[592,128]{1,0:T(8,128)S(1)}, f32[592,128]{1,0:T(8,128)S(1)}, u32[]{:S(2)}, u32[]{:S(2)}) %collective-permute-start.2) | collective-permute-done | bytes 303136 | tf_op jit(solution)/shard_map/ppermute | solution.py:115
  34.8 2.6 collective-permute-start.5
  38.9 6.1 %collective-permute-done.5.refs_2_ = f32[208,128]{1,0:T(8,128)S(1)} collective-permute-done((f32[208,128]{1,0:T(8,128)S(1)}, f32[208,128]{1,0:T(8,128)S(1)}, u32[]{:S(2)}, u32[]{:S(2)}) %collective-permute-start.5) | collective-permute-done | bytes 106528 | tf_op jit(solution)/shard_map/ppermute | solution.py:115
  49.8 3.6 %collective-permute-done.8 = f32[144,128]{1,0:T(8,128)S(1)} collective-permute-done((f32[144,128]{1,0:T(8,128)S(1)}, f32[144,128]{1,0:T(8,128)S(1)}, u32[]{:S(2)}, u32[]{:S(2)}) %collective-permute-start.8) | collective-permute-done | bytes 73760 | tf_op jit(solution)/shard_map/ppermute | solution.py:115
  58.0 5.3 %collective-permute-done.10.refs_5_ = f32[576,128]{1,0:T(8,128)S(1)} collective-permute-done((f32[576,128]{1,0:T(8,128)S(1)}, f32[576,128]{1,0:T(8,128)S(1)}, u32[]{:S(2)}, u32[]{:S(2)}) %collective-permute-start.10) | collective-permute-done | bytes 294944 | tf_op jit(solution)/shard_map/ppermute | solution.py:115
  63.3 4.5 %collective-permute-done.11.refs_6_ = f32[576,128]{1,0:T(8,128)S(1)} collective-permute-done((f32[576,128]{1,0:T(8,128)S(1)}, f32[576,128]{1,0:T(8,128)S(1)}, u32[]{:S(2)}, u32[]{:S(2)}) %collective-permute-start.11) | collective-permute-done | bytes 294944 | tf_op jit(solution)/shard_map/ppermute | solution.py:115
  69.8 65.5 %shard_map.62 = (f32[1024,1024]{1,0:T(8,128)}, f32[256,1024]{1,0:T(8,128)S(1)}, bf16[256,1024]{1,0:T(8,128)(2,1)}, f32[256,1024]{1,0:T(8,128)}, f32[2320,128]{1,0:T(8,128)}, /*index=5*/f32[2320,128]{1,0:T(8,128)}) custom-call(s32[1,1]{1,0:T(1,128)} %bitcast.pos_ref.refs_0_, f32[256,128]{1,0:T(8,128)S(1)} %get-tuple-element.46.refs_1_, ...), custom_call_target="tpu_custom_call" | custom-call | tf_op jit(solution)/shard_map/pallas_call | solution.py:399
  136.4 2.9 %collective-permute-done.17.refs_1_ = f32[2320,128]{1,0:T(8,128)S(1)} collective-permute-done((f32[2320,128]{1,0:T(8,128)}, f32[2320,128]{1,0:T(8,128)S(1)}, u32[]{:S(2)}, u32[]{:S(2)}) %collective-permute-start.17) | collective-permute-done | bytes 1187872 | tf_op jit(solution)/shard_map/ppermute | solution.py:115
  144.3 6.5 %collective-permute-done.18.refs_1_ = f32[592,128]{1,0:T(8,128)S(1)} collective-permute-done((f32[592,128]{1,0:T(8,128)S(1)}, f32[592,128]{1,0:T(8,128)S(1)}, u32[]{:S(2)}, u32[]{:S(2)}) %collective-permute-start.18) | collective-permute-done | bytes 303136 | tf_op jit(solution)/shard_map/ppermute | solution.py:115
  150.8 5.8 %collective-permute-done.19.refs_2_ = f32[592,128]{1,0:T(8,128)S(1)} collective-permute-done((f32[592,128]{1,0:T(8,128)S(1)}, f32[592,128]{1,0:T(8,128)S(1)}, u32[]{:S(2)}, u32[]{:S(2)}) %collective-permute-start.19) | collective-permute-done | bytes 303136 | tf_op jit(solution)/shard_map/ppermute | solution.py:115
  156.7 2.3 collective-permute-start.21
  159.4 2.1 collective-permute-start.23
  161.6 5.8 %collective-permute-done.22.refs_2_ = f32[160,128]{1,0:T(8,128)S(1)} collective-permute-done((f32[160,128]{1,0:T(8,128)S(1)}, f32[160,128]{1,0:T(8,128)S(1)}, u32[]{:S(2)}, u32[]{:S(2)}) %collective-permute-start.22) | collective-permute-done | bytes 81952 | tf_op jit(solution)/shard_map/ppermute | solution.py:115
  169.8 2.1 collective-permute-start.26
  173.2 3.2 %collective-permute-done.25 = f32[144,128]{1,0:T(8,128)S(1)} collective-permute-done((f32[144,128]{1,0:T(8,128)S(1)}, f32[144,128]{1,0:T(8,128)S(1)}, u32[]{:S(2)}, u32[]{:S(2)}) %collective-permute-start.25) | collective-permute-done | bytes 73760 | tf_op jit(solution)/shard_map/ppermute | solution.py:115
  180.0 5.6 %collective-permute-done.27.refs_6_ = f32[576,128]{1,0:T(8,128)S(1)} collective-permute-done((f32[576,128]{1,0:T(8,128)S(1)}, f32[576,128]{1,0:T(8,128)S(1)}, u32[]{:S(2)}, u32[]{:S(2)}) %collective-permute-start.27) | collective-permute-done | bytes 294944 | tf_op jit(solution)/shard_map/ppermute | solution.py:115
  185.5 4.5 %collective-permute-done.28.refs_7_ = f32[576,128]{1,0:T(8,128)S(1)} collective-permute-done((f32[576,128]{1,0:T(8,128)S(1)}, f32[576,128]{1,0:T(8,128)S(1)}, u32[]{:S(2)}, u32[]{:S(2)}) %collective-permute-start.28) | collective-permute-done | bytes 294944 | tf_op jit(solution)/shard_map/ppermute | solution.py:115
  192.1 8.1 %shard_map.67 = bf16[256,1024]{1,0:T(8,128)(2,1)S(1)} custom-call(s32[1,1]{1,0:T(1,128)} %bitcast.pos_ref.refs_0_, f32[16,128]{1,0:T(8,128)S(1)} %get-tuple-element.61.refs_1_, f32[256,1024]{1,0:T(8,128)S(1)} %copy-done.5, f32[256,1024]{1,0:T(8,128)} %copy-done.4, f32[1024,1024]{1,0:T(8,128)} %get-tuple-element.64.refs_4_, ...), custom_call_target="tpu_custom_call" | custom-call | tf_op jit(solution)/shard_map/pallas_call | solution.py:399
  202.8 2.1 collective-permute-done.37
  205.9 1.9 collective-permute-done.34
  208.9 21.7 %collective-permute-done.38 = f32[512,512]{0,1:T(8,128)S(1)} collective-permute-done((f32[512,512]{0,1:T(8,128)S(1)}, f32[512,512]{0,1:T(8,128)S(1)}, u32[]{:S(2)}, u32[]{:S(2)}) %collective-permute-start.38) | collective-permute-done | bytes 1048608 | tf_op jit(solution)/shard_map/ppermute | solution.py:115
  231.2 3.2 %collective-permute-done.35 = f32[512,512]{0,1:T(8,128)S(1)} collective-permute-done((f32[512,512]{0,1:T(8,128)S(1)}, f32[512,512]{0,1:T(8,128)S(1)}, u32[]{:S(2)}, u32[]{:S(2)}) %collective-permute-start.35) | collective-permute-done | bytes 1048608 | tf_op jit(solution)/shard_map/ppermute | solution.py:115
  235.1 9.7 %collective-permute-done.39 = f32[256,512]{0,1:T(8,128)S(1)} collective-permute-done((f32[256,512]{0,1:T(8,128)S(1)}, f32[256,512]{0,1:T(8,128)S(1)}, u32[]{:S(2)}, u32[]{:S(2)}) %collective-permute-start.39) | collective-permute-done | bytes 524320 | tf_op jit(solution)/shard_map/ppermute | solution.py:115
  245.1 1.9 collective-permute-done.36
  247.5 2.1 collective-permute-start.40
  252.0 2.3 convolution_convert_fusion
  254.3 13.9 %collective-permute-done.40 = f32[64,1024]{0,1:T(8,128)S(1)} collective-permute-done((f32[64,1024]{0,1:T(8,128)S(1)}, f32[64,1024]{0,1:T(8,128)S(1)}, u32[]{:S(2)}, u32[]{:S(2)}) %collective-permute-start.40) | collective-permute-done | bytes 262176 | tf_op jit(solution)/shard_map/ppermute | solution.py:115
  268.2 19.6 %collective-permute-done.41 = f32[64,1024]{0,1:T(8,128)S(1)} collective-permute-done((f32[64,1024]{0,1:T(8,128)S(1)}, f32[64,1024]{0,1:T(8,128)S(1)}, u32[]{:S(2)}, u32[]{:S(2)}) %collective-permute-start.41) | collective-permute-done | bytes 262176 | tf_op jit(solution)/shard_map/ppermute | solution.py:115
  (102 shorter events, 45.1 us)
Async XLA Ops:
  14.7 10.9 %collective-permute-start.1 = (f32[592,128]{1,0:T(8,128)S(1)}, f32[592,128]{1,0:T(8,128)S(1)}, u32[]{:S(2)}, u32[]{:S(2)}) collective-permute-start(f32[592,128]{1,0:T(8,128)S(1)} %get-tuple-element.39), channel_id=1, source_target_pairs={{0,8},{1,9},{2,10},{3,11},{4,12},{5,13},{6,14},{7,15},{8,0},{9,1},... | collective-permute-start | bytes 909320 | tf_op jit(solution)/shard_map/ppermute | solution.py:115
  17.6 15.4 %collective-permute-start.2 = (f32[592,128]{1,0:T(8,128)S(1)}, f32[592,128]{1,0:T(8,128)S(1)}, u32[]{:S(2)}, u32[]{:S(2)}) collective-permute-start(f32[592,128]{1,0:T(8,128)S(1)} %get-tuple-element.40), channel_id=1, source_target_pairs={{0,16},{1,17},{2,18},{3,19},{4,20},{5,21},{6,22},{7,23},{8,24},{9,... | collective-permute-start | bytes 909320 | tf_op jit(solution)/shard_map/ppermute | solution.py:115
  19.1 13.9 %collective-permute-start.3 = (f32[592,128]{1,0:T(8,128)S(1)}, f32[592,128]{1,0:T(8,128)S(1)}, u32[]{:S(2)}, u32[]{:S(2)}) collective-permute-start(f32[592,128]{1,0:T(8,128)S(1)} %get-tuple-element.41), channel_id=1, source_target_pairs={{0,24},{1,25},{2,26},{3,27},{4,28},{5,29},{6,30},{7,31},{8,16},{9,... | collective-permute-start | bytes 909320 | tf_op jit(solution)/shard_map/ppermute | solution.py:115
  33.1 5.8 %collective-permute-start.4 = (f32[208,128]{1,0:T(8,128)S(1)}, f32[208,128]{1,0:T(8,128)S(1)}, u32[]{:S(2)}, u32[]{:S(2)}) collective-permute-start(f32[208,128]{1,0:T(8,128)S(1)} %get-tuple-element.43), channel_id=1, source_target_pairs={{0,2},{1,3},{2,0},{3,1},{4,6},{5,7},{6,4},{7,5},{8,10},{9,11},{10,... | collective-permute-start | bytes 319496 | tf_op jit(solution)/shard_map/ppermute | solution.py:115
  34.8 10.3 %collective-permute-start.5 = (f32[208,128]{1,0:T(8,128)S(1)}, f32[208,128]{1,0:T(8,128)S(1)}, u32[]{:S(2)}, u32[]{:S(2)}) collective-permute-start(f32[208,128]{1,0:T(8,128)S(1)} %get-tuple-element.44), channel_id=1, source_target_pairs={{0,4},{1,5},{2,6},{3,7},{4,0},{5,1},{6,2},{7,3},{8,12},{9,13},{10,... | collective-permute-start | bytes 319496 | tf_op jit(solution)/shard_map/ppermute | solution.py:115
  37.4 7.7 %collective-permute-start.6 = (f32[208,128]{1,0:T(8,128)S(1)}, f32[208,128]{1,0:T(8,128)S(1)}, u32[]{:S(2)}, u32[]{:S(2)}) collective-permute-start(f32[208,128]{1,0:T(8,128)S(1)} %get-tuple-element.45), channel_id=1, source_target_pairs={{0,6},{1,7},{2,4},{3,5},{4,2},{5,3},{6,0},{7,1},{8,14},{9,15},{10,... | collective-permute-start | bytes 319496 | tf_op jit(solution)/shard_map/ppermute | solution.py:115
  46.9 6.5 %collective-permute-start.8 = (f32[144,128]{1,0:T(8,128)S(1)}, f32[144,128]{1,0:T(8,128)S(1)}, u32[]{:S(2)}, u32[]{:S(2)}) collective-permute-start(f32[144,128]{1,0:T(8,128)S(1)} %get-tuple-element.48), channel_id=1, source_target_pairs={{0,4},{1,5},{2,6},{3,7},{4,0},{5,1},{6,2},{7,3},{8,12},{9,13},{10,... | collective-permute-start | bytes 221192 | tf_op jit(solution)/shard_map/ppermute | solution.py:115
  48.2 6.3 %collective-permute-start.9 = (f32[144,128]{1,0:T(8,128)S(1)}, f32[144,128]{1,0:T(8,128)S(1)}, u32[]{:S(2)}, u32[]{:S(2)}) collective-permute-start(f32[144,128]{1,0:T(8,128)S(1)} %get-tuple-element.48), channel_id=1, source_target_pairs={{0,6},{1,7},{2,4},{3,5},{4,2},{5,3},{6,0},{7,1},{8,14},{9,15},{10,... | collective-permute-start | bytes 221192 | tf_op jit(solution)/shard_map/ppermute | solution.py:115
  54.5 8.8 %collective-permute-start.10 = (f32[576,128]{1,0:T(8,128)S(1)}, f32[576,128]{1,0:T(8,128)S(1)}, u32[]{:S(2)}, u32[]{:S(2)}) collective-permute-start(f32[576,128]{1,0:T(8,128)S(1)} %constant_dynamic-update-slice_fusion.refs_4_), channel_id=1, source_target_pairs={{0,8},{1,9},{2,10},{3,11},{4,12},{5,13},{6,14},{7,15},{8,0},{9,1},... | collective-permute-start | bytes 884744 | tf_op jit(solution)/shard_map/ppermute | solution.py:115
  55.9 11.9 %collective-permute-start.11 = (f32[576,128]{1,0:T(8,128)S(1)}, f32[576,128]{1,0:T(8,128)S(1)}, u32[]{:S(2)}, u32[]{:S(2)}) collective-permute-start(f32[576,128]{1,0:T(8,128)S(1)} %constant_dynamic-update-slice_fusion.refs_4_), channel_id=1, source_target_pairs={{0,16},{1,17},{2,18},{3,19},{4,20},{5,21},{6,22},{7,23},{8,24},{9,... | collective-permute-start | bytes 884744 | tf_op jit(solution)/shard_map/ppermute | solution.py:115
  56.5 11.3 %collective-permute-start.12 = (f32[576,128]{1,0:T(8,128)S(1)}, f32[576,128]{1,0:T(8,128)S(1)}, u32[]{:S(2)}, u32[]{:S(2)}) collective-permute-start(f32[576,128]{1,0:T(8,128)S(1)} %constant_dynamic-update-slice_fusion.refs_4_), channel_id=1, source_target_pairs={{0,24},{1,25},{2,26},{3,27},{4,28},{5,29},{6,30},{7,31},{8,16},{9,... | collective-permute-start | bytes 884744 | tf_op jit(solution)/shard_map/ppermute | solution.py:115
  58.0 10.3 %collective-permute-start.13 = (f32[576,128]{1,0:T(8,128)S(1)}, f32[576,128]{1,0:T(8,128)S(1)}, u32[]{:S(2)}, u32[]{:S(2)}) collective-permute-start(f32[576,128]{1,0:T(8,128)S(1)} %constant_dynamic-update-slice_fusion.refs_4_), channel_id=1, source_target_pairs={{0,1},{1,0},{2,3},{3,2},{4,5},{5,4},{6,7},{7,6},{8,9},{9,8},{10,11... | collective-permute-start | bytes 884744 | tf_op jit(solution)/shard_map/ppermute | solution.py:115
  140.7 10.1 %collective-permute-start.18 = (f32[592,128]{1,0:T(8,128)S(1)}, f32[592,128]{1,0:T(8,128)S(1)}, u32[]{:S(2)}, u32[]{:S(2)}) collective-permute-start(f32[592,128]{1,0:T(8,128)S(1)} %get-tuple-element.54), channel_id=1, source_target_pairs={{0,8},{1,9},{2,10},{3,11},{4,12},{5,13},{6,14},{7,15},{8,0},{9,1},... | collective-permute-start | bytes 909320 | tf_op jit(solution)/shard_map/ppermute | solution.py:115
  141.2 15.4 %collective-permute-start.19 = (f32[592,128]{1,0:T(8,128)S(1)}, f32[592,128]{1,0:T(8,128)S(1)}, u32[]{:S(2)}, u32[]{:S(2)}) collective-permute-start(f32[592,128]{1,0:T(8,128)S(1)} %get-tuple-element.55), channel_id=1, source_target_pairs={{0,16},{1,17},{2,18},{3,19},{4,20},{5,21},{6,22},{7,23},{8,24},{9,... | collective-permute-start | bytes 909320 | tf_op jit(solution)/shard_map/ppermute | solution.py:115
  142.8 13.9 %collective-permute-start.20 = (f32[592,128]{1,0:T(8,128)S(1)}, f32[592,128]{1,0:T(8,128)S(1)}, u32[]{:S(2)}, u32[]{:S(2)}) collective-permute-start(f32[592,128]{1,0:T(8,128)S(1)} %get-tuple-element.56), channel_id=1, source_target_pairs={{0,24},{1,25},{2,26},{3,27},{4,28},{5,29},{6,30},{7,31},{8,16},{9,... | collective-permute-start | bytes 909320 | tf_op jit(solution)/shard_map/ppermute | solution.py:115
  159.0 8.4 %collective-permute-start.22 = (f32[160,128]{1,0:T(8,128)S(1)}, f32[160,128]{1,0:T(8,128)S(1)}, u32[]{:S(2)}, u32[]{:S(2)}) collective-permute-start(f32[160,128]{1,0:T(8,128)S(1)} %get-tuple-element.59), channel_id=1, source_target_pairs={{0,4},{1,5},{2,6},{3,7},{4,0},{5,1},{6,2},{7,3},{8,12},{9,13},{10,... | collective-permute-start | bytes 245768 | tf_op jit(solution)/shard_map/ppermute | solution.py:115
  159.4 8.0 %collective-permute-start.23 = (f32[160,128]{1,0:T(8,128)S(1)}, f32[160,128]{1,0:T(8,128)S(1)}, u32[]{:S(2)}, u32[]{:S(2)}) collective-permute-start(f32[160,128]{1,0:T(8,128)S(1)} %get-tuple-element.60), channel_id=1, source_target_pairs={{0,6},{1,7},{2,4},{3,5},{4,2},{5,3},{6,0},{7,1},{8,14},{9,15},{10,... | collective-permute-start | bytes 245768 | tf_op jit(solution)/shard_map/ppermute | solution.py:115
  168.9 7.5 %collective-permute-start.25 = (f32[144,128]{1,0:T(8,128)S(1)}, f32[144,128]{1,0:T(8,128)S(1)}, u32[]{:S(2)}, u32[]{:S(2)}) collective-permute-start(f32[144,128]{1,0:T(8,128)S(1)} %get-tuple-element.65), channel_id=1, source_target_pairs={{0,4},{1,5},{2,6},{3,7},{4,0},{5,1},{6,2},{7,3},{8,12},{9,13},{10,... | collective-permute-start | bytes 221192 | tf_op jit(solution)/shard_map/ppermute | solution.py:115
  169.8 6.6 %collective-permute-start.26 = (f32[144,128]{1,0:T(8,128)S(1)}, f32[144,128]{1,0:T(8,128)S(1)}, u32[]{:S(2)}, u32[]{:S(2)}) collective-permute-start(f32[144,128]{1,0:T(8,128)S(1)} %get-tuple-element.65), channel_id=1, source_target_pairs={{0,6},{1,7},{2,4},{3,5},{4,2},{5,3},{6,0},{7,1},{8,14},{9,15},{10,... | collective-permute-start | bytes 221192 | tf_op jit(solution)/shard_map/ppermute | solution.py:115
  176.4 9.1 %collective-permute-start.27 = (f32[576,128]{1,0:T(8,128)S(1)}, f32[576,128]{1,0:T(8,128)S(1)}, u32[]{:S(2)}, u32[]{:S(2)}) collective-permute-start(f32[576,128]{1,0:T(8,128)S(1)} %constant_dynamic-update-slice_fusion.4.refs_5_), channel_id=1, source_target_pairs={{0,8},{1,9},{2,10},{3,11},{4,12},{5,13},{6,14},{7,15},{8,0},{9,1},... | collective-permute-start | bytes 884744 | tf_op jit(solution)/shard_map/ppermute | solution.py:115
  177.9 12.1 %collective-permute-start.28 = (f32[576,128]{1,0:T(8,128)S(1)}, f32[576,128]{1,0:T(8,128)S(1)}, u32[]{:S(2)}, u32[]{:S(2)}) collective-permute-start(f32[576,128]{1,0:T(8,128)S(1)} %constant_dynamic-update-slice_fusion.4.refs_5_), channel_id=1, source_target_pairs={{0,16},{1,17},{2,18},{3,19},{4,20},{5,21},{6,22},{7,23},{8,24},{9,... | collective-permute-start | bytes 884744 | tf_op jit(solution)/shard_map/ppermute | solution.py:115
  178.6 11.5 %collective-permute-start.29 = (f32[576,128]{1,0:T(8,128)S(1)}, f32[576,128]{1,0:T(8,128)S(1)}, u32[]{:S(2)}, u32[]{:S(2)}) collective-permute-start(f32[576,128]{1,0:T(8,128)S(1)} %constant_dynamic-update-slice_fusion.4.refs_5_), channel_id=1, source_target_pairs={{0,24},{1,25},{2,26},{3,27},{4,28},{5,29},{6,30},{7,31},{8,16},{9,... | collective-permute-start | bytes 884744 | tf_op jit(solution)/shard_map/ppermute | solution.py:115
  180.0 11.4 %collective-permute-start.30 = (f32[576,128]{1,0:T(8,128)S(1)}, f32[576,128]{1,0:T(8,128)S(1)}, u32[]{:S(2)}, u32[]{:S(2)}) collective-permute-start(f32[576,128]{1,0:T(8,128)S(1)} %constant_dynamic-update-slice_fusion.4.refs_5_), channel_id=1, source_target_pairs={{0,1},{1,0},{2,3},{3,2},{4,5},{5,4},{6,7},{7,6},{8,9},{9,8},{10,11... | collective-permute-start | bytes 884744 | tf_op jit(solution)/shard_map/ppermute | solution.py:115
  185.5 5.8 %collective-permute-start.31 = (f32[576,128]{1,0:T(8,128)S(1)}, f32[576,128]{1,0:T(8,128)S(1)}, u32[]{:S(2)}, u32[]{:S(2)}) collective-permute-start(f32[576,128]{1,0:T(8,128)S(1)} %collective-permute-done.27.refs_6_), channel_id=1, source_target_pairs={{0,1},{1,0},{2,3},{3,2},{4,5},{5,4},{6,7},{7,6},{8,9},{9,8},{10,11... | collective-permute-start | bytes 884744 | tf_op jit(solution)/shard_map/ppermute | solution.py:115
  201.3 6.5 %collective-permute-start.34 = (f32[1024,512]{0,1:T(8,128)S(1)}, f32[1024,512]{0,1:T(8,128)S(1)}, u32[]{:S(2)}, u32[]{:S(2)}) collective-permute-start(f32[1024,512]{0,1:T(8,128)S(1)} %fusion.12), channel_id=1, source_target_pairs={{0,1},{1,0},{2,3},{3,2},{4,5},{5,4},{6,7},{7,6},{8,9},{9,8},{10,11... | collective-permute-start | bytes 6291464 | tf_op jit(solution)/shard_map/ppermute | solution.py:115
  205.4 25.3 %collective-permute-start.38 = (f32[512,512]{0,1:T(8,128)S(1)}, f32[512,512]{0,1:T(8,128)S(1)}, u32[]{:S(2)}, u32[]{:S(2)}) collective-permute-start(f32[512,512]{0,1:T(8,128)S(1)} %get-tuple-element.75), channel_id=1, source_target_pairs={{0,16},{1,17},{2,18},{3,19},{4,20},{5,21},{6,22},{7,23},{8,24},{9,... | collective-permute-start | bytes 3145736 | tf_op jit(solution)/shard_map/ppermute | solution.py:115
  208.4 26.1 %collective-permute-start.35 = (f32[512,512]{0,1:T(8,128)S(1)}, f32[512,512]{0,1:T(8,128)S(1)}, u32[]{:S(2)}, u32[]{:S(2)}) collective-permute-start(f32[512,512]{0,1:T(8,128)S(1)} %get-tuple-element.73), channel_id=1, source_target_pairs={{0,8},{1,9},{2,10},{3,11},{4,12},{5,13},{6,14},{7,15},{8,0},{9,1},... | collective-permute-start | bytes 3145736 | tf_op jit(solution)/shard_map/ppermute | solution.py:115
  230.7 14.1 %collective-permute-start.39 = (f32[256,512]{0,1:T(8,128)S(1)}, f32[256,512]{0,1:T(8,128)S(1)}, u32[]{:S(2)}, u32[]{:S(2)}) collective-permute-start(f32[256,512]{0,1:T(8,128)S(1)} %slice_add_fusion.4), channel_id=1, source_target_pairs={{0,8},{1,9},{2,10},{3,11},{4,12},{5,13},{6,14},{7,15},{8,0},{9,1},... | collective-permute-start | bytes 1572872 | tf_op jit(solution)/shard_map/ppermute | solution.py:115
  234.5 12.4 %collective-permute-start.36 = (f32[256,512]{0,1:T(8,128)S(1)}, f32[256,512]{0,1:T(8,128)S(1)}, u32[]{:S(2)}, u32[]{:S(2)}) collective-permute-start(f32[256,512]{0,1:T(8,128)S(1)} %slice_add_fusion.6), channel_id=1, source_target_pairs={{0,16},{1,17},{2,18},{3,19},{4,20},{5,21},{6,22},{7,23},{8,24},{9,... | collective-permute-start | bytes 1572872 | tf_op jit(solution)/shard_map/ppermute | solution.py:115
  247.5 20.7 %collective-permute-start.40 = (f32[64,1024]{0,1:T(8,128)S(1)}, f32[64,1024]{0,1:T(8,128)S(1)}, u32[]{:S(2)}, u32[]{:S(2)}) collective-permute-start(f32[64,1024]{0,1:T(8,128)S(1)} %get-tuple-element.76), channel_id=1, source_target_pairs={{0,2},{1,3},{2,0},{3,1},{4,6},{5,7},{6,4},{7,5},{8,10},{9,11},{10,... | collective-permute-start | bytes 786440 | tf_op jit(solution)/shard_map/ppermute | solution.py:115
  249.6 38.2 %collective-permute-start.41 = (f32[64,1024]{0,1:T(8,128)S(1)}, f32[64,1024]{0,1:T(8,128)S(1)}, u32[]{:S(2)}, u32[]{:S(2)}) collective-permute-start(f32[64,1024]{0,1:T(8,128)S(1)} %get-tuple-element.78), channel_id=1, source_target_pairs={{0,4},{1,5},{2,6},{3,7},{4,0},{5,1},{6,2},{7,3},{8,12},{9,13},{10,... | collective-permute-start | bytes 786440 | tf_op jit(solution)/shard_map/ppermute | solution.py:115
  250.3 37.5 %collective-permute-start.42 = (f32[64,1024]{0,1:T(8,128)S(1)}, f32[64,1024]{0,1:T(8,128)S(1)}, u32[]{:S(2)}, u32[]{:S(2)}) collective-permute-start(f32[64,1024]{0,1:T(8,128)S(1)} %get-tuple-element.77), channel_id=1, source_target_pairs={{0,6},{1,7},{2,4},{3,5},{4,2},{5,3},{6,0},{7,1},{8,14},{9,15},{10,... | collective-permute-start | bytes 786440 | tf_op jit(solution)/shard_map/ppermute | solution.py:115
  (19 other events, 206.0 us)
